TPU v7x, 32 devices: a whole 2x2x4 slice. The times are simulated.
32 devices in a mesh: dp: 16 (over z, y, x), rep: 2 (over core).
Axes of the slice: x: 2, y: 2, z: 4, core: 2. Of those that a mesh axis runs over, the one named last changes fastest.
Arguments:
- queries: bfloat16 [32768, 1024], P(('dp', 'rep')), may hold values from -12 to 12
- keys: bfloat16 [2048, 1024], P('dp'), may hold values from -5 to 5
- neg_mask: int32 [256, 16], P(('dp', 'rep')), may hold values from 0 to 1, as said below
- positive: int32 [256], P(('dp', 'rep')), may hold values from 0 to 15, as said below
- row_weight: float32 [32768], P(('dp', 'rep')), may hold values from 2 to 20
Outputs:
- row_loss: float32 [32768], P(('dp', 'rep'))
- grad_queries: float32 [32768, 1024], P(('dp', 'rep'))
- grad_keys: float32 [2048, 1024], P(('dp', 'rep'))
Inputs may be any that keep to these rules, and one draw needn't show every extreme that they name: neg_mask[b, c] is 0 unless key block c lies at cyclic distance at most 4 from the dp index that holds query block b (query blocks numbered along dp+rep, 8 to a device); for every b the two key blocks at distance exactly 4 are 1. positive[b] lies at cyclic distance at most 4 from the dp index that holds query block b.
All inputs are finite; a program needn't handle non-finite values.
Results may differ from a plain program's by a relative error of at most 0.003.
Values may be sent and summed in bfloat16 or wider, within the bound.
A program may use at most 128 MiB of HBM per device.

v0:
```python
import math

import jax
import jax.numpy as jnp
from jax import lax
from jax.sharding import PartitionSpec as P

D = 1024
REACH = 4


def passed_along(x, axis, by):
    count = lax.axis_size(axis)
    return lax.ppermute(x, axis, [(i, (i + by) % count) for i in range(count)])


def body(queries, keys, neg_mask, positive, row_weight):
    logit_scale = 2.0 / math.sqrt(D)
    cycle_size = lax.axis_size("dp")
    cycle_index = lax.axis_index("dp")
    query_rows = queries.shape[0]
    tile_rows = keys.shape[0]
    query_blocks = query_rows // tile_rows
    inner_idx = jnp.arange(tile_rows, dtype=jnp.int32)
    same_row = inner_idx[:, None] == inner_idx[None, :]
    key_tiles = [(0, keys)]
    upward = keys
    downward = keys
    for hop_count in range(1, REACH + 1):
        upward = passed_along(upward, "dp", 1)
        downward = passed_along(downward, "dp", -1)
        key_tiles.append((hop_count, upward))
        key_tiles.append((-hop_count, downward))
    run_max = jnp.full((query_rows,), -1e30, jnp.float32)
    run_sum = jnp.zeros((query_rows,), jnp.float32)
    pos_logit = jnp.zeros((query_rows,), jnp.float32)
    stored = []
    for distance, key_tile in key_tiles:
        owner_idx = (cycle_index - distance) % cycle_size
        column = lax.dynamic_slice_in_dim(neg_mask, owner_idx, 1, 1)[:, 0]
        hit_block = positive == owner_idx
        allow_block = (column == 1) | hit_block
        allowed = jnp.broadcast_to(
            allow_block[:, None, None], (query_blocks, tile_rows, tile_rows)
        ).reshape(query_rows, tile_rows)
        at_positive = (hit_block[:, None, None] & same_row[None, :, :]).reshape(
            query_rows, tile_rows
        )
        allowed, at_positive = (allowed, at_positive)
        logit_tile = logit_scale * lax.dot_general(
            queries, key_tile, (((1,), (1,)), ((), ())), preferred_element_type=jnp.float32
        )
        masked = jnp.where(allowed, logit_tile, jnp.float32(-1e30))
        next_max = jnp.maximum(run_max, jnp.max(masked, axis=1))
        run_sum = run_sum * jnp.exp(run_max - next_max) + jnp.sum(
            jnp.where(allowed, jnp.exp(masked - next_max[:, None]), 0.0), axis=1
        )
        run_max = next_max
        pos_logit = pos_logit + jnp.sum(jnp.where(at_positive, logit_tile, 0.0), axis=1)
        stored.append((distance, key_tile, masked, at_positive))
    log_total = run_max + jnp.log(run_sum)
    row_loss = log_total - pos_logit
    grad_query = jnp.zeros(queries.shape, jnp.float32)
    key_parts = {}
    for distance, key_tile, masked, at_positive in stored:
        softmax_p = jnp.exp(masked - log_total[:, None])
        coefficient = (row_weight[:, None] * (softmax_p - at_positive.astype(jnp.float32))).astype(
            jnp.bfloat16
        )
        grad_query = grad_query + logit_scale * jnp.dot(
            coefficient, key_tile, preferred_element_type=jnp.float32
        )
        key_parts[distance] = logit_scale * lax.dot_general(
            coefficient, queries, (((0,), (0,)), ((), ())), preferred_element_type=jnp.float32
        )
    upward = jnp.zeros_like(key_parts[0])
    for distance in range(REACH, 0, -1):
        upward = passed_along(upward + key_parts[distance], "dp", -1)
    downward = jnp.zeros_like(key_parts[0])
    for distance in range(-REACH, 0):
        downward = passed_along(downward + key_parts[distance], "dp", 1)
    grad_keys = lax.psum_scatter(
        key_parts[0] + upward + downward, "rep", scatter_dimension=0, tiled=True
    )
    return (row_loss, grad_query, grad_keys)


def solution(mesh):
    placed = (
        P(("dp", "rep"), None),
        P("dp", None),
        P(("dp", "rep"), None),
        P(("dp", "rep")),
        P(("dp", "rep")),
    )
    return jax.shard_map(
        body,
        mesh=mesh,
        in_specs=placed,
        out_specs=(P(("dp", "rep")), P(("dp", "rep"), None), P(("dp", "rep"), None)),
        check_vma=False,
    )
```

profile of v0, /device:TPU:0, one launch (start us, length us, event | category | flops | bytes accessed | tf_op | source)
XLA Modules:
  0.0 184.5 jit_solution(2349657084342050153)
XLA Ops:
  7.2 3.0 %collective-permute-start = (bf16[128,1024]{1,0:T(8,128)(2,1)}, bf16[128,1024]{1,0:T(8,128)(2,1)S(1)}, u32[]{:S(2)}, u32[]{:S(2)}) collective-permute-start(bf16[128,1024]{1,0:T(8,128)(2,1)} %param.6), channel_id=1, source_target_pairs={{0,2},{2,4},{4,6},{6,8},{8,10},{10,12},{12,14},{14,16},{16,18},{18... | collective-permute-start | bytes 786440 | tf_op jit(solution)/shard_map/ppermute | solution.py:14
  10.2 4.1 %collective-permute-start.1 = (bf16[128,1024]{1,0:T(8,128)(2,1)}, bf16[128,1024]{1,0:T(8,128)(2,1)S(1)}, u32[]{:S(2)}, u32[]{:S(2)}) collective-permute-start(bf16[128,1024]{1,0:T(8,128)(2,1)} %param.6), channel_id=1, source_target_pairs={{0,30},{2,0},{4,2},{6,4},{8,6},{10,8},{12,10},{14,12},{16,14},{18,... | collective-permute-start | bytes 786440 | tf_op jit(solution)/shard_map/ppermute | solution.py:14
  14.3 0.6 iota_compare_fusion
  14.9 1.3 fusion.10
  16.2 0.7 fusion.48
  17.0 0.1 broadcast_bitcast_fusion.16
  17.1 0.1 broadcast_bitcast_fusion.8
  17.1 0.1 broadcast_bitcast_fusion.10
  17.6 1.8 select_reduce_fusion.26
  19.5 2.3 %collective-permute-done = bf16[128,1024]{1,0:T(8,128)(2,1)S(1)} collective-permute-done((bf16[128,1024]{1,0:T(8,128)(2,1)}, bf16[128,1024]{1,0:T(8,128)(2,1)S(1)}, u32[]{:S(2)}, u32[]{:S(2)}) %collective-permute-start) | collective-permute-done | bytes 262176 | tf_op jit(solution)/shard_map/ppermute | solution.py:14
  21.7 2.4 %collective-permute-start.2 = (bf16[128,1024]{1,0:T(8,128)(2,1)S(1)}, bf16[128,1024]{1,0:T(8,128)(2,1)S(1)}, u32[]{:S(2)}, u32[]{:S(2)}) collective-permute-start(bf16[128,1024]{1,0:T(8,128)(2,1)S(1)} %collective-permute-done), channel_id=1, source_target_pairs={{0,2},{2,4},{4,6},{6,8},{8,10},{10,12},{12,14},{14,16},{16,18},{18... | collective-permute-start | bytes 786440 | tf_op jit(solution)/shard_map/ppermute | solution.py:14
  24.1 3.2 %collective-permute-start.3 = (bf16[128,1024]{1,0:T(8,128)(2,1)S(1)}, bf16[128,1024]{1,0:T(8,128)(2,1)S(1)}, u32[]{:S(2)}, u32[]{:S(2)}) collective-permute-start(bf16[128,1024]{1,0:T(8,128)(2,1)S(1)} %collective-permute-done.1), channel_id=1, source_target_pairs={{0,30},{2,0},{4,2},{6,4},{8,6},{10,8},{12,10},{14,12},{16,14},{18,... | collective-permute-start | bytes 786440 | tf_op jit(solution)/shard_map/ppermute | solution.py:14
  27.3 0.8 select_reduce_fusion.24
  28.2 0.8 select_reduce_fusion.25
  29.0 5.4 %collective-permute-done.2 = bf16[128,1024]{1,0:T(8,128)(2,1)S(1)} collective-permute-done((bf16[128,1024]{1,0:T(8,128)(2,1)S(1)}, bf16[128,1024]{1,0:T(8,128)(2,1)S(1)}, u32[]{:S(2)}, u32[]{:S(2)}) %collective-permute-start.2) | collective-permute-done | bytes 262176 | tf_op jit(solution)/shard_map/ppermute | solution.py:14
  34.4 2.5 %collective-permute-start.4 = (bf16[128,1024]{1,0:T(8,128)(2,1)S(1)}, bf16[128,1024]{1,0:T(8,128)(2,1)S(1)}, u32[]{:S(2)}, u32[]{:S(2)}) collective-permute-start(bf16[128,1024]{1,0:T(8,128)(2,1)S(1)} %collective-permute-done.2), channel_id=1, source_target_pairs={{0,2},{2,4},{4,6},{6,8},{8,10},{10,12},{12,14},{14,16},{16,18},{18... | collective-permute-start | bytes 786440 | tf_op jit(solution)/shard_map/ppermute | solution.py:14
  36.9 4.7 %collective-permute-start.5 = (bf16[128,1024]{1,0:T(8,128)(2,1)S(1)}, bf16[128,1024]{1,0:T(8,128)(2,1)S(1)}, u32[]{:S(2)}, u32[]{:S(2)}) collective-permute-start(bf16[128,1024]{1,0:T(8,128)(2,1)S(1)} %collective-permute-done.3), channel_id=1, source_target_pairs={{0,30},{2,0},{4,2},{6,4},{8,6},{10,8},{12,10},{14,12},{16,14},{18,... | collective-permute-start | bytes 786440 | tf_op jit(solution)/shard_map/ppermute | solution.py:14
  41.6 0.8 select_reduce_fusion.22
  42.4 0.8 select_reduce_fusion.23
  43.3 3.0 %collective-permute-done.4 = bf16[128,1024]{1,0:T(8,128)(2,1)S(1)} collective-permute-done((bf16[128,1024]{1,0:T(8,128)(2,1)S(1)}, bf16[128,1024]{1,0:T(8,128)(2,1)S(1)}, u32[]{:S(2)}, u32[]{:S(2)}) %collective-permute-start.4) | collective-permute-done | bytes 262176 | tf_op jit(solution)/shard_map/ppermute | solution.py:14
  46.3 2.5 %collective-permute-start.6 = (bf16[128,1024]{1,0:T(8,128)(2,1)S(1)}, bf16[128,1024]{1,0:T(8,128)(2,1)S(1)}, u32[]{:S(2)}, u32[]{:S(2)}) collective-permute-start(bf16[128,1024]{1,0:T(8,128)(2,1)S(1)} %collective-permute-done.4), channel_id=1, source_target_pairs={{0,2},{2,4},{4,6},{6,8},{8,10},{10,12},{12,14},{14,16},{16,18},{18... | collective-permute-start | bytes 786440 | tf_op jit(solution)/shard_map/ppermute | solution.py:14
  48.8 6.6 %collective-permute-start.7 = (bf16[128,1024]{1,0:T(8,128)(2,1)S(1)}, bf16[128,1024]{1,0:T(8,128)(2,1)S(1)}, u32[]{:S(2)}, u32[]{:S(2)}) collective-permute-start(bf16[128,1024]{1,0:T(8,128)(2,1)S(1)} %collective-permute-done.5), channel_id=1, source_target_pairs={{0,30},{2,0},{4,2},{6,4},{8,6},{10,8},{12,10},{14,12},{16,14},{18,... | collective-permute-start | bytes 786440 | tf_op jit(solution)/shard_map/ppermute | solution.py:14
  55.3 0.8 select_reduce_fusion.20
  56.2 0.8 select_reduce_fusion.21
  57.0 4.1 %collective-permute-done.7 = bf16[128,1024]{1,0:T(8,128)(2,1)S(1)} collective-permute-done((bf16[128,1024]{1,0:T(8,128)(2,1)S(1)}, bf16[128,1024]{1,0:T(8,128)(2,1)S(1)}, u32[]{:S(2)}, u32[]{:S(2)}) %collective-permute-start.7) | collective-permute-done | bytes 262176 | tf_op jit(solution)/shard_map/ppermute | solution.py:14
  61.1 0.8 select_reduce_fusion.18
  61.9 0.8 select_reduce_fusion.19
  62.9 0.2 select_reduce_fusion.6
  63.1 0.8 select_reduce_fusion.8
  63.9 0.8 select_reduce_fusion.7
  64.7 0.6 add_subtract_fusion
  65.4 0.5 convolution_multiply_fusion.7
  65.9 0.5 convolution_multiply_fusion.3
  66.4 0.4 copy-done.2
  66.9 2.7 %fusion.12 = f32[1024,1024]{1,0:T(8,128)} fusion(bf16[128,1024]{1,0:T(8,128)(2,1)S(1)} %copy-done.2, f32[1024,128]{0,1:T(8,128)S(1)} %get-tuple-element.104, f32[1024]{0:T(1024)S(1)} %get-tuple-element.43, f32[1024]{0:T(1024)S(1)} %copy-done.1, pred[1024]{0:T(1024)(128)(4,1)S(1)} %get-tuple-element.113, pred[1024]{0:T(1024)(128)(4,1)S(1)} %get-tuple-element.122, ...), kind=kOutput, calls=%fused_computation.117 | convolution fusion | flops 269352960 | bytes 5122048 | tf_op jit(solution)/shard_map/dot_general | solution.py:70
  69.6 6.2 %collective-permute-start.8 = (f32[128,1024]{1,0:T(8,128)S(1)}, f32[128,1024]{1,0:T(8,128)S(1)}, u32[]{:S(2)}, u32[]{:S(2)}) collective-permute-start(f32[128,1024]{1,0:T(8,128)S(1)} %convolution_multiply_fusion.7), channel_id=1, source_target_pairs={{0,30},{2,0},{4,2},{6,4},{8,6},{10,8},{12,10},{14,12},{16,14},{18,... | collective-permute-start | bytes 1572872 | tf_op jit(solution)/shard_map/ppermute | solution.py:14
  75.8 2.7 %fusion.17 = f32[1024,1024]{1,0:T(8,128)} fusion(bf16[128,1024]{1,0:T(8,128)(2,1)S(1)} %collective-permute-done.4, f32[1024,128]{0,1:T(8,128)S(1)} %get-tuple-element.94, f32[1024]{0:T(1024)S(1)} %get-tuple-element.43, f32[1024]{0:T(1024)S(1)} %copy-done.1, pred[1024]{0:T(1024)(128)(4,1)S(1)} %get-tuple-element.108, ...), kind=kOutput, calls=%fused_computation.122 | convolution fusion | flops 269352960 | bytes 5122048 | tf_op jit(solution)/shard_map/dot_general | solution.py:70
  78.5 2.7 %fusion.18 = f32[1024,1024]{1,0:T(8,128)} fusion(bf16[128,1024]{1,0:T(8,128)(2,1)S(1)} %collective-permute-done.5, f32[1024,128]{0,1:T(8,128)S(1)} %get-tuple-element.92, f32[1024]{0:T(1024)S(1)} %get-tuple-element.43, f32[1024]{0:T(1024)S(1)} %copy-done.1, pred[1024]{0:T(1024)(128)(4,1)S(1)} %get-tuple-element.107, ...), kind=kOutput, calls=%fused_computation.123 | convolution fusion | flops 269352960 | bytes 5122048 | tf_op jit(solution)/shard_map/dot_general | solution.py:70
  81.2 2.7 %fusion.13 = f32[1024,1024]{1,0:T(8,128)} fusion(bf16[128,1024]{1,0:T(8,128)(2,1)S(1)} %collective-permute-done, f32[1024,128]{0,1:T(8,128)S(1)} %get-tuple-element.102, f32[1024]{0:T(1024)S(1)} %get-tuple-element.43, f32[1024]{0:T(1024)S(1)} %copy-done.1, pred[1024]{0:T(1024)(128)(4,1)S(1)} %get-tuple-element.112, ...), kind=kOutput, calls=%fused_computation.118 | convolution fusion | flops 269352960 | bytes 5122048 | tf_op jit(solution)/shard_map/dot_general | solution.py:70
  83.9 2.7 %fusion.14 = f32[1024,1024]{1,0:T(8,128)} fusion(bf16[128,1024]{1,0:T(8,128)(2,1)S(1)} %collective-permute-done.1, f32[1024,128]{0,1:T(8,128)S(1)} %get-tuple-element.100, f32[1024]{0:T(1024)S(1)} %get-tuple-element.43, f32[1024]{0:T(1024)S(1)} %copy-done.1, pred[1024]{0:T(1024)(128)(4,1)S(1)} %get-tuple-element.111, ...), kind=kOutput, calls=%fused_computation.119 | convolution fusion | flops 269352960 | bytes 5122048 | tf_op jit(solution)/shard_map/dot_general | solution.py:70
  86.6 0.5 convolution_multiply_fusion.1
  87.1 0.5 convolution_multiply_fusion.5
  87.6 4.0 %collective-permute-done.12 = f32[128,1024]{1,0:T(8,128)S(1)} collective-permute-done((f32[128,1024]{1,0:T(8,128)S(1)}, f32[128,1024]{1,0:T(8,128)S(1)}, u32[]{:S(2)}, u32[]{:S(2)}) %collective-permute-start.12) | collective-permute-done | bytes 524320 | tf_op jit(solution)/shard_map/ppermute | solution.py:14
  91.6 0.5 fusion
  92.1 2.5 %collective-permute-start.13 = (f32[128,1024]{1,0:T(8,128)S(1)}, f32[128,1024]{1,0:T(8,128)S(1)}, u32[]{:S(2)}, u32[]{:S(2)}) collective-permute-start(f32[128,1024]{1,0:T(8,128)S(1)} %fusion), channel_id=1, source_target_pairs={{0,2},{2,4},{4,6},{6,8},{8,10},{10,12},{12,14},{14,16},{16,18},{18... | collective-permute-start | bytes 1572872 | tf_op jit(solution)/shard_map/ppermute | solution.py:14
  94.7 1.0 collective-permute-done.8
  95.6 0.5 fusion.1
  96.2 4.5 %collective-permute-start.9 = (f32[128,1024]{1,0:T(8,128)S(1)}, f32[128,1024]{1,0:T(8,128)S(1)}, u32[]{:S(2)}, u32[]{:S(2)}) collective-permute-start(f32[128,1024]{1,0:T(8,128)S(1)} %fusion.1), channel_id=1, source_target_pairs={{0,30},{2,0},{4,2},{6,4},{8,6},{10,8},{12,10},{14,12},{16,14},{18,... | collective-permute-start | bytes 1572872 | tf_op jit(solution)/shard_map/ppermute | solution.py:14
  100.7 0.5 convolution_multiply_fusion
  101.2 2.7 %fusion.15 = f32[1024,1024]{1,0:T(8,128)} fusion(bf16[128,1024]{1,0:T(8,128)(2,1)S(1)} %collective-permute-done.2, f32[1024,128]{0,1:T(8,128)S(1)} %get-tuple-element.98, f32[1024]{0:T(1024)S(1)} %get-tuple-element.43, f32[1024]{0:T(1024)S(1)} %copy-done.1, pred[1024]{0:T(1024)(128)(4,1)S(1)} %get-tuple-element.110, ...), kind=kOutput, calls=%fused_computation.120 | convolution fusion | flops 269352960 | bytes 5122048 | tf_op jit(solution)/shard_map/dot_general | solution.py:70
  103.9 12.0 %collective-permute-done.13 = f32[128,1024]{1,0:T(8,128)S(1)} collective-permute-done((f32[128,1024]{1,0:T(8,128)S(1)}, f32[128,1024]{1,0:T(8,128)S(1)}, u32[]{:S(2)}, u32[]{:S(2)}) %collective-permute-start.13) | collective-permute-done | bytes 524320 | tf_op jit(solution)/shard_map/ppermute | solution.py:14
  116.0 2.5 %collective-permute-start.14 = (f32[128,1024]{1,0:T(8,128)S(1)}, f32[128,1024]{1,0:T(8,128)S(1)}, u32[]{:S(2)}, u32[]{:S(2)}) collective-permute-start(f32[128,1024]{1,0:T(8,128)S(1)} %add.264), channel_id=1, source_target_pairs={{0,2},{2,4},{4,6},{6,8},{8,10},{10,12},{12,14},{14,16},{16,18},{18... | collective-permute-start | bytes 1572872 | tf_op jit(solution)/shard_map/ppermute | solution.py:14
  118.6 6.5 %collective-permute-start.10 = (f32[128,1024]{1,0:T(8,128)S(1)}, f32[128,1024]{1,0:T(8,128)S(1)}, u32[]{:S(2)}, u32[]{:S(2)}) collective-permute-start(f32[128,1024]{1,0:T(8,128)S(1)} %add.260), channel_id=1, source_target_pairs={{0,30},{2,0},{4,2},{6,4},{8,6},{10,8},{12,10},{14,12},{16,14},{18,... | collective-permute-start | bytes 1572872 | tf_op jit(solution)/shard_map/ppermute | solution.py:14
  125.1 0.5 convolution_multiply_fusion.4
  125.6 2.7 %fusion.16 = f32[1024,1024]{1,0:T(8,128)} fusion(bf16[128,1024]{1,0:T(8,128)(2,1)S(1)} %collective-permute-done.3, f32[1024,128]{0,1:T(8,128)S(1)} %get-tuple-element.96, f32[1024]{0:T(1024)S(1)} %get-tuple-element.43, f32[1024]{0:T(1024)S(1)} %copy-done.1, pred[1024]{0:T(1024)(128)(4,1)S(1)} %get-tuple-element.109, ...), kind=kOutput, calls=%fused_computation.121 | convolution fusion | flops 269352960 | bytes 5122048 | tf_op jit(solution)/shard_map/dot_general | solution.py:70
  128.3 11.1 %collective-permute-done.14 = f32[128,1024]{1,0:T(8,128)S(1)} collective-permute-done((f32[128,1024]{1,0:T(8,128)S(1)}, f32[128,1024]{1,0:T(8,128)S(1)}, u32[]{:S(2)}, u32[]{:S(2)}) %collective-permute-start.14) | collective-permute-done | bytes 524320 | tf_op jit(solution)/shard_map/ppermute | solution.py:14
  139.5 2.5 %collective-permute-start.15 = (f32[128,1024]{1,0:T(8,128)S(1)}, f32[128,1024]{1,0:T(8,128)S(1)}, u32[]{:S(2)}, u32[]{:S(2)}) collective-permute-start(f32[128,1024]{1,0:T(8,128)S(1)} %add.265), channel_id=1, source_target_pairs={{0,2},{2,4},{4,6},{6,8},{8,10},{10,12},{12,14},{14,16},{16,18},{18... | collective-permute-start | bytes 1572872 | tf_op jit(solution)/shard_map/ppermute | solution.py:14
  142.1 6.4 %collective-permute-start.11 = (f32[128,1024]{1,0:T(8,128)S(1)}, f32[128,1024]{1,0:T(8,128)S(1)}, u32[]{:S(2)}, u32[]{:S(2)}) collective-permute-start(f32[128,1024]{1,0:T(8,128)S(1)} %add.261), channel_id=1, source_target_pairs={{0,30},{2,0},{4,2},{6,4},{8,6},{10,8},{12,10},{14,12},{16,14},{18,... | collective-permute-start | bytes 1572872 | tf_op jit(solution)/shard_map/ppermute | solution.py:14
  148.5 0.5 convolution_multiply_fusion.8
  149.0 2.8 %fusion.19 = f32[1024,1024]{1,0:T(8,128)} fusion(bf16[128,1024]{1,0:T(8,128)(2,1)S(1)} %collective-permute-done.6, f32[1024,128]{0,1:T(8,128)S(1)} %get-tuple-element.90, f32[1024]{0:T(1024)S(1)} %get-tuple-element.43, f32[1024]{0:T(1024)S(1)} %copy-done.1, pred[1024]{0:T(1024)(128)(4,1)S(1)} %get-tuple-element.106, ...), kind=kOutput, calls=%fused_computation.124 | convolution fusion | flops 269352960 | bytes 5122048 | tf_op jit(solution)/shard_map/dot_general | solution.py:70
  151.8 10.3 %collective-permute-done.15 = f32[128,1024]{1,0:T(8,128)S(1)} collective-permute-done((f32[128,1024]{1,0:T(8,128)S(1)}, f32[128,1024]{1,0:T(8,128)S(1)}, u32[]{:S(2)}, u32[]{:S(2)}) %collective-permute-start.15) | collective-permute-done | bytes 524320 | tf_op jit(solution)/shard_map/ppermute | solution.py:14
  162.1 0.7 collective-permute-done.11
  162.8 0.9 add_add_fusion
  163.8 13.9 %add_multiply_fusion = f32[1024,1024]{1,0:T(8,128)} fusion(f32[1024,1024]{1,0:T(8,128)} %fusion.19, f32[1024,1024]{1,0:T(8,128)} %fusion.18, f32[1024,1024]{1,0:T(8,128)} %fusion.17, f32[1024,1024]{1,0:T(8,128)} %fusion.16, f32[1024,1024]{1,0:T(8,128)} %fusion.15, f32[1024,1024]{1,0:T(8,128)} %fusion.14, f32[1024,1024]{1,0:T(8,128)} %fusion.12, ...), kind=kOutput, calls=%fused_computation | convolution fusion | flops 278790144 | bytes 38676480 | tf_op jit(solution)/shard_map/dot_general | solution.py:70
  (29 shorter events, 0.9 us)
Async XLA Ops:
  7.2 10.5 %copy-start = (bf16[1024,1024]{1,0:T(8,128)(2,1)S(1)}, bf16[1024,1024]{1,0:T(8,128)(2,1)}, u32[]{:S(2)}) copy-start(bf16[1024,1024]{1,0:T(8,128)(2,1)} %param.5) | copy-start | bytes 6291460
  7.2 170.5 %reduce-scatter.2.cloned.1.call-start = ((), (), s32[]{:S(2)}) async-start(), calls=%async_computation.1 | async-start | bytes 786432 | tf_op jit(solution)/shard_map/reduce_scatter | solution.py:82
  7.2 14.5 %collective-permute-start = (bf16[128,1024]{1,0:T(8,128)(2,1)}, bf16[128,1024]{1,0:T(8,128)(2,1)S(1)}, u32[]{:S(2)}, u32[]{:S(2)}) collective-permute-start(bf16[128,1024]{1,0:T(8,128)(2,1)} %param.6), channel_id=1, source_target_pairs={{0,2},{2,4},{4,6},{6,8},{8,10},{10,12},{12,14},{14,16},{16,18},{18... | collective-permute-start | bytes 786440 | tf_op jit(solution)/shard_map/ppermute | solution.py:14
  10.2 13.9 %collective-permute-start.1 = (bf16[128,1024]{1,0:T(8,128)(2,1)}, bf16[128,1024]{1,0:T(8,128)(2,1)S(1)}, u32[]{:S(2)}, u32[]{:S(2)}) collective-permute-start(bf16[128,1024]{1,0:T(8,128)(2,1)} %param.6), channel_id=1, source_target_pairs={{0,30},{2,0},{4,2},{6,4},{8,6},{10,8},{12,10},{14,12},{16,14},{18,... | collective-permute-start | bytes 786440 | tf_op jit(solution)/shard_map/ppermute | solution.py:14
  21.7 12.7 %collective-permute-start.2 = (bf16[128,1024]{1,0:T(8,128)(2,1)S(1)}, bf16[128,1024]{1,0:T(8,128)(2,1)S(1)}, u32[]{:S(2)}, u32[]{:S(2)}) collective-permute-start(bf16[128,1024]{1,0:T(8,128)(2,1)S(1)} %collective-permute-done), channel_id=1, source_target_pairs={{0,2},{2,4},{4,6},{6,8},{8,10},{10,12},{12,14},{14,16},{16,18},{18... | collective-permute-start | bytes 786440 | tf_op jit(solution)/shard_map/ppermute | solution.py:14
  24.1 12.8 %collective-permute-start.3 = (bf16[128,1024]{1,0:T(8,128)(2,1)S(1)}, bf16[128,1024]{1,0:T(8,128)(2,1)S(1)}, u32[]{:S(2)}, u32[]{:S(2)}) collective-permute-start(bf16[128,1024]{1,0:T(8,128)(2,1)S(1)} %collective-permute-done.1), channel_id=1, source_target_pairs={{0,30},{2,0},{4,2},{6,4},{8,6},{10,8},{12,10},{14,12},{16,14},{18,... | collective-permute-start | bytes 786440 | tf_op jit(solution)/shard_map/ppermute | solution.py:14
  34.4 11.9 %collective-permute-start.4 = (bf16[128,1024]{1,0:T(8,128)(2,1)S(1)}, bf16[128,1024]{1,0:T(8,128)(2,1)S(1)}, u32[]{:S(2)}, u32[]{:S(2)}) collective-permute-start(bf16[128,1024]{1,0:T(8,128)(2,1)S(1)} %collective-permute-done.2), channel_id=1, source_target_pairs={{0,2},{2,4},{4,6},{6,8},{8,10},{10,12},{12,14},{14,16},{16,18},{18... | collective-permute-start | bytes 786440 | tf_op jit(solution)/shard_map/ppermute | solution.py:14
  36.9 11.9 %collective-permute-start.5 = (bf16[128,1024]{1,0:T(8,128)(2,1)S(1)}, bf16[128,1024]{1,0:T(8,128)(2,1)S(1)}, u32[]{:S(2)}, u32[]{:S(2)}) collective-permute-start(bf16[128,1024]{1,0:T(8,128)(2,1)S(1)} %collective-permute-done.3), channel_id=1, source_target_pairs={{0,30},{2,0},{4,2},{6,4},{8,6},{10,8},{12,10},{14,12},{16,14},{18,... | collective-permute-start | bytes 786440 | tf_op jit(solution)/shard_map/ppermute | solution.py:14
  46.3 15.7 %collective-permute-start.6 = (bf16[128,1024]{1,0:T(8,128)(2,1)S(1)}, bf16[128,1024]{1,0:T(8,128)(2,1)S(1)}, u32[]{:S(2)}, u32[]{:S(2)}) collective-permute-start(bf16[128,1024]{1,0:T(8,128)(2,1)S(1)} %collective-permute-done.4), channel_id=1, source_target_pairs={{0,2},{2,4},{4,6},{6,8},{8,10},{10,12},{12,14},{14,16},{16,18},{18... | collective-permute-start | bytes 786440 | tf_op jit(solution)/shard_map/ppermute | solution.py:14
  48.8 12.3 %collective-permute-start.7 = (bf16[128,1024]{1,0:T(8,128)(2,1)S(1)}, bf16[128,1024]{1,0:T(8,128)(2,1)S(1)}, u32[]{:S(2)}, u32[]{:S(2)}) collective-permute-start(bf16[128,1024]{1,0:T(8,128)(2,1)S(1)} %collective-permute-done.5), channel_id=1, source_target_pairs={{0,30},{2,0},{4,2},{6,4},{8,6},{10,8},{12,10},{14,12},{16,14},{18,... | collective-permute-start | bytes 786440 | tf_op jit(solution)/shard_map/ppermute | solution.py:14
  61.9 0.9 copy-start.3
  63.1 2.2 %copy-start.1 = (f32[1024]{0:T(1024)S(1)}, f32[1024]{0:T(1024)}, u32[]{:S(2)}) copy-start(f32[1024]{0:T(1024)} %param.9) | copy-start | bytes 12292
  65.9 1.0 copy-start.2
  69.6 22.0 %collective-permute-start.12 = (f32[128,1024]{1,0:T(8,128)S(1)}, f32[128,1024]{1,0:T(8,128)S(1)}, u32[]{:S(2)}, u32[]{:S(2)}) collective-permute-start(f32[128,1024]{1,0:T(8,128)S(1)} %convolution_multiply_fusion.3), channel_id=1, source_target_pairs={{0,2},{2,4},{4,6},{6,8},{8,10},{10,12},{12,14},{14,16},{16,18},{18... | collective-permute-start | bytes 1572872 | tf_op jit(solution)/shard_map/ppermute | solution.py:14
  69.6 26.1 %collective-permute-start.8 = (f32[128,1024]{1,0:T(8,128)S(1)}, f32[128,1024]{1,0:T(8,128)S(1)}, u32[]{:S(2)}, u32[]{:S(2)}) collective-permute-start(f32[128,1024]{1,0:T(8,128)S(1)} %convolution_multiply_fusion.7), channel_id=1, source_target_pairs={{0,30},{2,0},{4,2},{6,4},{8,6},{10,8},{12,10},{14,12},{16,14},{18,... | collective-permute-start | bytes 1572872 | tf_op jit(solution)/shard_map/ppermute | solution.py:14
  92.1 23.8 %collective-permute-start.13 = (f32[128,1024]{1,0:T(8,128)S(1)}, f32[128,1024]{1,0:T(8,128)S(1)}, u32[]{:S(2)}, u32[]{:S(2)}) collective-permute-start(f32[128,1024]{1,0:T(8,128)S(1)} %fusion), channel_id=1, source_target_pairs={{0,2},{2,4},{4,6},{6,8},{8,10},{10,12},{12,14},{14,16},{16,18},{18... | collective-permute-start | bytes 1572872 | tf_op jit(solution)/shard_map/ppermute | solution.py:14
  96.2 22.4 %collective-permute-start.9 = (f32[128,1024]{1,0:T(8,128)S(1)}, f32[128,1024]{1,0:T(8,128)S(1)}, u32[]{:S(2)}, u32[]{:S(2)}) collective-permute-start(f32[128,1024]{1,0:T(8,128)S(1)} %fusion.1), channel_id=1, source_target_pairs={{0,30},{2,0},{4,2},{6,4},{8,6},{10,8},{12,10},{14,12},{16,14},{18,... | collective-permute-start | bytes 1572872 | tf_op jit(solution)/shard_map/ppermute | solution.py:14
  116.0 23.5 %collective-permute-start.14 = (f32[128,1024]{1,0:T(8,128)S(1)}, f32[128,1024]{1,0:T(8,128)S(1)}, u32[]{:S(2)}, u32[]{:S(2)}) collective-permute-start(f32[128,1024]{1,0:T(8,128)S(1)} %add.264), channel_id=1, source_target_pairs={{0,2},{2,4},{4,6},{6,8},{8,10},{10,12},{12,14},{14,16},{16,18},{18... | collective-permute-start | bytes 1572872 | tf_op jit(solution)/shard_map/ppermute | solution.py:14
  118.6 23.5 %collective-permute-start.10 = (f32[128,1024]{1,0:T(8,128)S(1)}, f32[128,1024]{1,0:T(8,128)S(1)}, u32[]{:S(2)}, u32[]{:S(2)}) collective-permute-start(f32[128,1024]{1,0:T(8,128)S(1)} %add.260), channel_id=1, source_target_pairs={{0,30},{2,0},{4,2},{6,4},{8,6},{10,8},{12,10},{14,12},{16,14},{18,... | collective-permute-start | bytes 1572872 | tf_op jit(solution)/shard_map/ppermute | solution.py:14
  139.5 22.6 %collective-permute-start.15 = (f32[128,1024]{1,0:T(8,128)S(1)}, f32[128,1024]{1,0:T(8,128)S(1)}, u32[]{:S(2)}, u32[]{:S(2)}) collective-permute-start(f32[128,1024]{1,0:T(8,128)S(1)} %add.265), channel_id=1, source_target_pairs={{0,2},{2,4},{4,6},{6,8},{8,10},{10,12},{12,14},{14,16},{16,18},{18... | collective-permute-start | bytes 1572872 | tf_op jit(solution)/shard_map/ppermute | solution.py:14
  142.1 20.7 %collective-permute-start.11 = (f32[128,1024]{1,0:T(8,128)S(1)}, f32[128,1024]{1,0:T(8,128)S(1)}, u32[]{:S(2)}, u32[]{:S(2)}) collective-permute-start(f32[128,1024]{1,0:T(8,128)S(1)} %add.261), channel_id=1, source_target_pairs={{0,30},{2,0},{4,2},{6,4},{8,6},{10,8},{12,10},{14,12},{16,14},{18,... | collective-permute-start | bytes 1572872 | tf_op jit(solution)/shard_map/ppermute | solution.py:14
Sparse Core Ops, SparseCore 0:
  163.9 8.8 reduce-scatter.1
where the time goes:
time: 185 us
  starting transfers between devices  60.1 us (32%)
  waiting for transfers between devices  53.8 us (29%)
  matrix products  48.9 us (26%)
  between operations  14.3 us (8%)
  other arithmetic  6.3 us (3%)
    ppermute x16, starting transfers between devices, passed_along(): return lax.ppermute(x, axis, [(i, (i + by) % count) for i in range(count)])  60 us
    ppermute x16, waiting for transfers between devices, passed_along(): return lax.ppermute(x, axis, [(i, (i + by) % count) for i in range(count)])  53.8 us
    dot_general x9, matrix products, body(): jnp.dot(coefficient, key_tile, preferred_element_type=jnp.float32)  35.7 us
    dot_general x9, matrix products, body(): lax.dot_general(queries, key_tile, (((1,), (1,)), ((), ())), preferred_el...  8.53 us
    dot_general x9, matrix products, body(): lax.dot_general(coefficient, queries, (((0,), (0,)), ((), ())), preferred...  4.67 us
  transfers between devices with their start and end apart: 17, of which 10 were waited for; matrix products, arithmetic and copies ran while one was open for 26% of the time, Pallas kernels for 0%

commit v1 on v0

v1 whole, which is shorter than its diff:
```python
import functools
import math

import jax
import jax.numpy as jnp
from jax import lax
from jax.experimental import pallas as pl
from jax.experimental.pallas import tpu as pltpu
from jax.sharding import PartitionSpec as P

REACH = 4
NEG = -1e30


def kernel(n, q_hbm, k_hbm, mask, positive, weight, loss, gq_hbm, gk_out,
           q, kwin, e, coef, gk, sib, outb, inb, gq, run_max, run_sum, pos_logit, hist,
           local_sem, g_send, g_recv, f_send, f_recv, x_send, x_recv, s_send, s_recv, o_sem):
    rows, width = q.shape
    blocks, tile = weight.shape
    half = tile // 2
    scale = 2.0 / math.sqrt(width)
    d = lax.axis_index("dp")
    r = lax.axis_index("rep")
    other = 1 - r

    def dev(by):
        return lax.rem(d + by + n, n)

    def owner_of(p):
        j = (p + 1) // 2
        return dev(jnp.where(p % 2 == 1, j, -j) if not isinstance(p, int) else (j if p % 2 else -j))

    q_copy = pltpu.make_async_copy(q_hbm, q, local_sem.at[0])
    q_copy.start()
    own = [
        pltpu.make_async_copy(k_hbm.at[pl.ds(h * half, half)], kwin.at[0, h], local_sem.at[1 + h])
        for h in range(2)
    ]
    for c in own:
        c.start()

    barrier = pltpu.get_barrier_semaphore()
    for by in range(1, REACH + 1):
        for sign in (1, -1):
            pl.semaphore_signal(barrier, inc=1, device_id={"dp": dev(sign * by)},
                                device_id_type=pl.DeviceIdType.MESH)
    pl.semaphore_signal(barrier, inc=1, device_id={"rep": other},
                        device_id_type=pl.DeviceIdType.MESH)
    pl.semaphore_wait(barrier, 2 * REACH + 1)

    def gather(p_dst, by):
        return pltpu.make_async_remote_copy(
            src_ref=k_hbm.at[pl.ds(pl.multiple_of(r * half, half), half)],
            dst_ref=kwin.at[p_dst, r],
            send_sem=g_send.at[p_dst], recv_sem=g_recv.at[p_dst],
            device_id={"dp": dev(by)}, device_id_type=pl.DeviceIdType.MESH)

    def forward(p, h):
        return pltpu.make_async_remote_copy(
            src_ref=kwin.at[p, h], dst_ref=kwin.at[p, h],
            send_sem=f_send.at[p], recv_sem=f_recv.at[p],
            device_id={"rep": other}, device_id_type=pl.DeviceIdType.MESH)

    for j in range(1, REACH + 1):
        gather(2 * j, j).start()
        gather(2 * j - 1, -j).start()

    run_max[...] = jnp.full(run_max.shape, NEG, jnp.float32)
    run_sum[...] = jnp.zeros(run_sum.shape, jnp.float32)
    pos_logit[...] = jnp.zeros(pos_logit.shape, jnp.float32)
    eye = (lax.broadcasted_iota(jnp.int32, (tile, tile), 0)
           == lax.broadcasted_iota(jnp.int32, (tile, tile), 1))
    eye_f = eye.astype(jnp.float32)

    def chunk(j, owners, first, count):
        k = kwin[pl.ds(first, count)].reshape(count * tile, width)
        group = 2 if blocks % 2 == 0 else 1
        for g in range(blocks // group):
            logit = lax.dot_general(
                k, q[g * group * tile:(g + 1) * group * tile, :],
                (((1,), (1,)), ((), ())), preferred_element_type=jnp.float32)
            for bb in range(group):
                b = g * group + bb
                lanes = slice(bb * tile, (bb + 1) * tile)
                old = run_max[b:b + 1, :]
                top = old
                masked = []
                found = pos_logit[b:b + 1, :]
                for i in range(count):
                    part = logit[i * tile:(i + 1) * tile, lanes] * scale
                    hit = positive[b] == owners[i]
                    allow = (mask[b, owners[i]] == 1) | hit
                    found = found + jnp.where(hit, 1.0, 0.0) * jnp.sum(
                        jnp.where(eye, part, 0.0), axis=0, keepdims=True)
                    part = part + jnp.where(allow, 0.0, NEG)
                    masked.append(part)
                    top = jnp.maximum(top, jnp.max(part, axis=0, keepdims=True))
                total = run_sum[b:b + 1, :] * jnp.exp(old - top)
                for i in range(count):
                    ex = jnp.exp(masked[i] - top)
                    total = total + jnp.sum(ex, axis=0, keepdims=True)
                    e[first + i, :, b * tile:(b + 1) * tile] = ex
                run_max[b:b + 1, :] = top
                run_sum[b:b + 1, :] = total
                pos_logit[b:b + 1, :] = found
        hist[j] = run_max[...]

    q_copy.wait()
    for c in own:
        c.wait()
    chunk(0, [d], 0, 1)

    @pl.loop(1, REACH + 1)
    def _(j):
        for p in (2 * j - 1, 2 * j):
            gather(p, 0).wait_recv()
            forward(p, r).start()
        for p in (2 * j - 1, 2 * j):
            forward(p, other).wait_recv()
        chunk(j, [dev(j), dev(-j)], 2 * j - 1, 2)

    log_total = run_max[...] + jnp.log(run_sum[...])
    loss[...] = log_total - pos_logit[...]
    w_over = weight[...] / run_sum[...]

    def finish(j, owners, first):
        factor = w_over * jnp.exp(hist[j] - run_max[...])
        for b in range(blocks):
            lanes = slice(b * tile, (b + 1) * tile)
            for i, owner in enumerate(owners):
                at = jnp.where(positive[b] == owner, 1.0, 0.0) * weight[b:b + 1, :]
                coef[first + i, :, lanes] = (
                    e[first + i, :, lanes] * factor[b:b + 1, :] - at * eye_f
                ).astype(jnp.bfloat16)

    def exchange(p, h):
        return pltpu.make_async_remote_copy(
            src_ref=gk.at[p, h], dst_ref=sib.at[p],
            send_sem=x_send.at[p], recv_sem=x_recv.at[p],
            device_id={"rep": other}, device_id_type=pl.DeviceIdType.MESH)

    def scatter(p, p_dst, to):
        return pltpu.make_async_remote_copy(
            src_ref=outb.at[p], dst_ref=inb.at[p_dst],
            send_sem=s_send.at[p], recv_sem=s_recv.at[p_dst],
            device_id={"dp": to}, device_id_type=pl.DeviceIdType.MESH)

    def key_grad(first, count):
        c = coef[pl.ds(first, count)].reshape(count * tile, rows)
        for g in range(4):
            cols = slice(g * (width // 4), (g + 1) * (width // 4))
            part = scale * jnp.dot(c, q[:, cols], preferred_element_type=jnp.float32)
            gk[pl.ds(first, count), :, :, cols] = part.reshape(count, 2, half, width // 4)

    def ship(j):
        for p, p_dst, by in ((2 * j - 1, 2 * j, j), (2 * j, 2 * j - 1, -j)):
            exchange(p, other).wait_recv()
            outb[p] = (gk[p, r] + sib[p]).astype(jnp.bfloat16)
            scatter(p, p_dst, dev(by)).start()

    @pl.loop(0, REACH)
    def _(i):
        j = REACH - i
        finish(j, [dev(j), dev(-j)], 2 * j - 1)
        key_grad(2 * j - 1, 2)
        for p in (2 * j - 1, 2 * j):
            exchange(p, other).start()

        @pl.when(i > 0)
        def _():
            ship(j + 1)

    finish(0, [d], 0)
    key_grad(0, 1)
    exchange(0, other).start()
    ship(1)

    k_all = kwin[...].reshape((2 * REACH + 1) * tile, width)
    c_all = coef
    step = rows // 4
    for g in range(4):
        ct = c_all[:, :, g * step:(g + 1) * step].reshape((2 * REACH + 1) * tile, step)
        gq[g * step:(g + 1) * step, :] = scale * lax.dot_general(
            ct, k_all, (((0,), (0,)), ((), ())), preferred_element_type=jnp.float32)
        pltpu.make_async_copy(gq.at[pl.ds(g * step, step)], gq_hbm.at[pl.ds(g * step, step)],
                              o_sem.at[g]).start()

    exchange(0, other).wait_recv()
    acc = gk[0, r] + sib[0]
    for p in range(1, 2 * REACH + 1):
        scatter(p, p, d).wait_recv()
        acc = acc + inb[p].astype(jnp.float32)
    gk_out[...] = acc

    for g in range(4):
        pltpu.make_async_copy(gq.at[pl.ds(g * step, step)], gq_hbm.at[pl.ds(g * step, step)],
                              o_sem.at[g]).wait()
    exchange(0, other).wait_send()
    for p in range(1, 2 * REACH + 1):
        gather(p, 0).wait_send()
        forward(p, r).wait_send()
        exchange(p, other).wait_send()
        scatter(p, p, d).wait_send()


def body(queries, keys, neg_mask, positive, row_weight):
    n = lax.axis_size("dp")
    rows, width = queries.shape
    tile = keys.shape[0]
    blocks = rows // tile
    half = tile // 2
    slots = 2 * REACH + 1
    any_, vmem, smem = (pl.BlockSpec(memory_space=m) for m in (pl.ANY, pltpu.VMEM, pltpu.SMEM))
    f32, bf16 = jnp.float32, jnp.bfloat16
    dma = pltpu.SemaphoreType.DMA
    loss, gq, gk = pl.pallas_call(
        functools.partial(kernel, n),
        out_shape=(
            jax.ShapeDtypeStruct((blocks, tile), f32),
            jax.ShapeDtypeStruct((rows, width), f32),
            jax.ShapeDtypeStruct((half, width), f32),
        ),
        in_specs=[any_, any_, smem, smem, vmem],
        out_specs=(vmem, any_, vmem),
        scratch_shapes=[
            pltpu.VMEM((rows, width), bf16),
            pltpu.VMEM((slots, 2, half, width), bf16),
            pltpu.VMEM((slots, tile, rows), f32),
            pltpu.VMEM((slots, tile, rows), bf16),
            pltpu.VMEM((slots, 2, half, width), f32),
            pltpu.VMEM((slots, half, width), f32),
            pltpu.VMEM((slots, half, width), bf16),
            pltpu.VMEM((slots, half, width), bf16),
            pltpu.VMEM((rows, width), f32),
            pltpu.VMEM((blocks, tile), f32),
            pltpu.VMEM((blocks, tile), f32),
            pltpu.VMEM((blocks, tile), f32),
            pltpu.VMEM((REACH + 1, blocks, tile), f32),
            dma((3,)),
            dma((slots,)), dma((slots,)), dma((slots,)), dma((slots,)),
            dma((slots,)), dma((slots,)), dma((slots,)), dma((slots,)),
            dma((4,)),
        ],
        compiler_params=pltpu.CompilerParams(
            collective_id=0, has_side_effects=True, vmem_limit_bytes=48 * 1024 * 1024),
        cost_estimate=pl.CostEstimate(
            flops=6 * rows * slots * tile * width, bytes_accessed=8 * rows * width,
            transcendentals=rows * slots * tile),
    )(queries, keys, neg_mask, positive, row_weight.reshape(blocks, tile))
    return loss.reshape(rows), gq, gk


def solution(mesh):
    placed = (
        P(("dp", "rep"), None),
        P("dp", None),
        P(("dp", "rep"), None),
        P(("dp", "rep")),
        P(("dp", "rep")),
    )
    return jax.shard_map(
        body,
        mesh=mesh,
        in_specs=placed,
        out_specs=(P(("dp", "rep")), P(("dp", "rep"), None), P(("dp", "rep"), None)),
        check_vma=False,
    )
```

time: 185 us -> 62.4 us (0.34)
  starting transfers between devices: 60.1 us -> 0 us
  waiting for transfers between devices: 53.8 us -> 0 us
  Pallas kernels: 0 us -> 50.8 us
  matrix products: 48.9 us -> 0 us
  between operations: 14.3 us -> 0.65 us
  local copies, waits for them, and re-layouts: 1.16 us -> 10.6 us
  other arithmetic: 6.3 us -> 0 us
    ppermute x16 -> x0, starting transfers between devices: 60 us -> none  [passed_along(): return lax.ppermute(x, axis, [(i, (i + by) % count) for i in range(count)])]
    ppermute x16 -> x0, waiting for transfers between devices: 53.8 us -> none  [passed_along(): return lax.ppermute(x, axis, [(i, (i + by) % count) for i in range(count)])]
    pallas_call x0 -> x1, Pallas kernels: none -> 50.8 us  [body(): pl.pallas_call(functools.partial(kernel, n), out_shape=(jax.ShapeDtypeStr...]
    dot_general x27 -> x0, matrix products: 48.9 us -> none  [the longest x9 35.7 us: body(): jnp.dot(coefficient, key_tile, preferred_element_type=jnp.float32)]
    unnamed x8 -> x13, local copies, waits for them, and re-layouts: 0.44 us -> 10.6 us
    eq x2 -> x0, other arithmetic: 1.97 us -> none  [the longest x1 1.35 us: body(): allow_block = (column == 1) | hit_block]
  transfers between devices with their start and end apart: 17 -> 0, of which waited for: 10 -> 0; matrix products, arithmetic and copies ran while one was open for 26% -> 0% of each run, Pallas kernels for 0% -> 0%
where the time goes in v1:
time: 62.4 us; the launch traced here: 62.1 us
  Pallas kernels  50.8 us (81%)
  local copies, waits for them, and re-layouts  10.6 us (17%)
  between operations  0.65 us (1%)
    pallas_call x1, Pallas kernels, body(): pl.pallas_call(functools.partial(kernel, n), out_shape=(jax.ShapeDtypeStr...  50.8 us
    unnamed x13, local copies, waits for them, and re-layouts  10.6 us

profile of v1, /device:TPU:0, one launch (start us, length us, event | category | flops | bytes accessed | tf_op | source)
XLA Modules:
  0.0 62.1 jit_solution(17410357099754572842)
XLA Ops:
  0.6 0.0 copy-start
  0.6 1.6 %copy-done = bf16[1024,1024]{1,0:T(8,128)(2,1)S(1)} copy-done((bf16[1024,1024]{1,0:T(8,128)(2,1)S(1)}, bf16[1024,1024]{1,0:T(8,128)(2,1)}, u32[]{:S(2)}) %copy-start) | copy-done | bytes 2097176
  2.2 0.0 copy-start.1
  2.2 0.9 %copy-done.1 = bf16[128,1024]{1,0:T(8,128)(2,1)S(1)} copy-done((bf16[128,1024]{1,0:T(8,128)(2,1)S(1)}, bf16[128,1024]{1,0:T(8,128)(2,1)}, u32[]{:S(2)}) %copy-start.1) | copy-done | bytes 262168
  3.2 0.0 copy-start.2
  3.2 0.7 %copy-done.2 = s32[8,16]{1,0:T(8,128)S(1)} copy-done((s32[8,16]{1,0:T(8,128)S(1)}, s32[8,16]{1,0:T(8,128)}, u32[]{:S(2)}) %copy-start.2) | copy-done | bytes 536
  3.9 0.0 copy-start.3
  3.9 0.7 %copy-done.3 = f32[1024]{0:T(1024)S(1)} copy-done((f32[1024]{0:T(1024)S(1)}, f32[1024]{0:T(1024)}, u32[]{:S(2)}) %copy-start.3) | copy-done | bytes 4120
  4.5 0.0 copy-start.4
  4.6 0.7 %copy-done.4 = s32[8]{0:T(128)S(1)} copy-done((s32[8]{0:T(128)S(1)}, s32[8]{0:T(128)}, u32[]{:S(2)}) %copy-start.4) | copy-done | bytes 56
  5.2 50.8 %shard_map.76 = (f32[8,128]{1,0:T(8,128)S(1)}, f32[1024,1024]{1,0:T(8,128)}, f32[64,1024]{1,0:T(8,128)S(1)}) custom-call(bf16[1024,1024]{1,0:T(8,128)(2,1)S(1)} %copy-done, bf16[128,1024]{1,0:T(8,128)(2,1)S(1)} %copy-done.1, s32[8,16]{1,0:T(8,128)S(1)} %copy-done.2, s32[8]{0:T(128)S(1)} %copy-done.4, f32[8,128]{1,0:T(8,128)S(1)} %bitcast.3), custom_call_target="tpu_custom_call" | custom-call | flops 7247757312 | bytes 8388608 | tf_op jit(solution)/shard_map/pallas_call | solution.py:216
  56.0 0.6 copy.11
  56.6 4.8 %copy.12 = f32[1024,1024]{1,0:T(8,128)} copy(f32[1024,1024]{1,0:T(8,128)} %get-tuple-element.13) | data formatting | bytes 8388608
  61.4 0.7 %copy.13 = f32[64,1024]{1,0:T(8,128)} copy(f32[64,1024]{1,0:T(8,128)S(1)} %get-tuple-element.14) | data formatting | bytes 524288
Async XLA Ops:
  0.6 1.6 %copy-start = (bf16[1024,1024]{1,0:T(8,128)(2,1)S(1)}, bf16[1024,1024]{1,0:T(8,128)(2,1)}, u32[]{:S(2)}) copy-start(bf16[1024,1024]{1,0:T(8,128)(2,1)} %q_hbm.1) | copy-start | bytes 6291460
  2.2 0.9 %copy-start.1 = (bf16[128,1024]{1,0:T(8,128)(2,1)S(1)}, bf16[128,1024]{1,0:T(8,128)(2,1)}, u32[]{:S(2)}) copy-start(bf16[128,1024]{1,0:T(8,128)(2,1)} %k_hbm.1) | copy-start | bytes 786436
  3.2 0.7 %copy-start.2 = (s32[8,16]{1,0:T(8,128)S(1)}, s32[8,16]{1,0:T(8,128)}, u32[]{:S(2)}) copy-start(s32[8,16]{1,0:T(8,128)} %mask.1) | copy-start | bytes 1540
  3.9 0.7 %copy-start.3 = (f32[1024]{0:T(1024)S(1)}, f32[1024]{0:T(1024)}, u32[]{:S(2)}) copy-start(f32[1024]{0:T(1024)} %param.9) | copy-start | bytes 12292
  4.5 0.7 %copy-start.4 = (s32[8]{0:T(128)S(1)}, s32[8]{0:T(128)}, u32[]{:S(2)}) copy-start(s32[8]{0:T(128)} %positive.1) | copy-start | bytes 100

commit v2 on v1

v2 whole, which is shorter than its diff:
```python
import functools
import math

import jax
import jax.numpy as jnp
from jax import lax
from jax.experimental import pallas as pl
from jax.experimental.pallas import tpu as pltpu
from jax.sharding import PartitionSpec as P

REACH = 4
GROUP = 4
NEG = -1e30


def kernel(n, q_hbm, k_hbm, mask_hbm, pos_hbm, weight_hbm, loss, gq, gk_out,
           mask, positive, weight, q, kwin, e, coef, gk, sib, outb, inb, run_max, run_sum, pos_logit, hist,
           local_sem, g_send, g_recv, f_send, f_recv, x_send, x_recv, s_send, s_recv):
    rows, width = q.shape
    blocks, tile = weight.shape
    half = tile // 2
    scale = 2.0 / math.sqrt(width)
    d = lax.axis_index("dp")
    r = lax.axis_index("rep")
    other = 1 - r

    def dev(by):
        return lax.rem(d + by + n, n)

    r4 = lax.rem(d, GROUP)
    base = d - r4
    even = 1 - 2 * lax.rem(r4, 2)
    place = [r4, r4 + even, lax.rem(r4 + 2, GROUP), GROUP - 1 - r4]
    mate = [base + c for c in place]

    def wrap(t):
        return lax.rem(t + n, n)

    owners = mate + [wrap(d + REACH), wrap(d - REACH)] + [
        wrap(mate[k] + jnp.where(place[k] < r4, REACH, -REACH)) for k in (1, 2, 3)]

    q_copy = pltpu.make_async_copy(q_hbm, q, local_sem.at[0])
    q_copy.start()
    own = [
        pltpu.make_async_copy(k_hbm.at[pl.ds(h * half, half)], kwin.at[0, h], local_sem.at[1 + h])
        for h in range(2)
    ]
    own += [
        pltpu.make_async_copy(src, dst, local_sem.at[3 + i])
        for i, (src, dst) in enumerate(
            ((mask_hbm, mask), (pos_hbm, positive), (weight_hbm, weight)))
    ]
    for c in own:
        c.start()

    barrier = pltpu.get_barrier_semaphore()
    for to in mate[1:] + [dev(REACH), dev(-REACH)]:
        pl.semaphore_signal(barrier, inc=1, device_id={"dp": to},
                            device_id_type=pl.DeviceIdType.MESH)
    pl.semaphore_signal(barrier, inc=1, device_id={"rep": other},
                        device_id_type=pl.DeviceIdType.MESH)
    pl.semaphore_wait(barrier, GROUP + 2)

    def gather(p, to):
        return pltpu.make_async_remote_copy(
            src_ref=k_hbm.at[pl.ds(pl.multiple_of(r * half, half), half)],
            dst_ref=kwin.at[p, r],
            send_sem=g_send.at[p], recv_sem=g_recv.at[p],
            device_id={"dp": to}, device_id_type=pl.DeviceIdType.MESH)

    def relay(src, k):
        return pltpu.make_async_remote_copy(
            src_ref=kwin.at[src, r], dst_ref=kwin.at[REACH + 1 + k, r],
            send_sem=g_send.at[REACH + 1 + k], recv_sem=g_recv.at[REACH + 1 + k],
            device_id={"dp": mate[k]}, device_id_type=pl.DeviceIdType.MESH)

    def pass_on(src):
        gather(src, d).wait_recv()
        for k in (1, 2, 3):
            @pl.when(jnp.where(place[k] > r4, REACH, REACH + 1) == src)
            def _():
                relay(src, k).start()
        forward(src, r).start()

    def forward(p, h):
        return pltpu.make_async_remote_copy(
            src_ref=kwin.at[p, h], dst_ref=kwin.at[p, h],
            send_sem=f_send.at[p], recv_sem=f_recv.at[p],
            device_id={"rep": other}, device_id_type=pl.DeviceIdType.MESH)

    gather(REACH + 1, dev(REACH)).start()
    gather(REACH, dev(-REACH)).start()
    for k in (1, 2, 3):
        gather(k, mate[k]).start()

    run_max[...] = jnp.full(run_max.shape, NEG, jnp.float32)
    run_sum[...] = jnp.zeros(run_sum.shape, jnp.float32)
    pos_logit[...] = jnp.zeros(pos_logit.shape, jnp.float32)
    eye = (lax.broadcasted_iota(jnp.int32, (tile, tile), 0)
           == lax.broadcasted_iota(jnp.int32, (tile, tile), 1))
    eye_f = eye.astype(jnp.float32)

    def chunk(j, owner, first, count):
        k = kwin[pl.ds(first, count)].reshape(count * tile, width)
        group = 2 if blocks % 2 == 0 else 1
        for g in range(blocks // group):
            logit = lax.dot_general(
                k, q[g * group * tile:(g + 1) * group * tile, :],
                (((1,), (1,)), ((), ())), preferred_element_type=jnp.float32)
            for bb in range(group):
                b = g * group + bb
                lanes = slice(bb * tile, (bb + 1) * tile)
                old = run_max[b:b + 1, :]
                top = old
                masked = []
                found = pos_logit[b:b + 1, :]
                for i in range(count):
                    part = logit[i * tile:(i + 1) * tile, lanes] * scale
                    hit = positive[b] == owner[i]
                    allow = (mask[b, owner[i]] == 1) | hit
                    found = found + jnp.where(hit, 1.0, 0.0) * jnp.sum(
                        jnp.where(eye, part, 0.0), axis=0, keepdims=True)
                    part = part + jnp.where(allow, 0.0, NEG)
                    masked.append(part)
                    top = jnp.maximum(top, jnp.max(part, axis=0, keepdims=True))
                total = run_sum[b:b + 1, :] * jnp.exp(old - top)
                for i in range(count):
                    ex = jnp.exp(masked[i] - top)
                    total = total + jnp.sum(ex, axis=0, keepdims=True)
                    e[first + i, :, b * tile:(b + 1) * tile] = ex
                run_max[b:b + 1, :] = top
                run_sum[b:b + 1, :] = total
                pos_logit[b:b + 1, :] = found
        hist[j] = run_max[...]

    q_copy.wait()
    for c in own:
        c.wait()
    chunk(0, owners[:1], 0, 1)

    def pick(p):
        out = owners[-1]
        for i in range(2 * REACH):
            out = jnp.where(p == i, owners[i], out)
        return out

    near = jnp.where(d + REACH < n, REACH, REACH + 1)
    pass_on(near)

    @pl.loop(1, REACH + 1)
    def _(j):
        pair = (2 * j - 1, 2 * j)

        @pl.when(j == 2)
        def _():
            pass_on(2 * REACH + 1 - near)

        for p in pair:
            @pl.when((p != REACH) & (p != REACH + 1))
            def _():
                gather(p, d).wait_recv()
                forward(p, r).start()
        for p in pair:
            forward(p, other).wait_recv()
        chunk(j, [pick(p) for p in pair], 2 * j - 1, 2)

    log_total = run_max[...] + jnp.log(run_sum[...])
    loss[...] = log_total - pos_logit[...]
    w_over = weight[...] / run_sum[...]

    def finish(j, owner, first):
        factor = w_over * jnp.exp(hist[j] - run_max[...])
        for b in range(blocks):
            lanes = slice(b * tile, (b + 1) * tile)
            for i, o in enumerate(owner):
                at = jnp.where(positive[b] == o, 1.0, 0.0) * weight[b:b + 1, :]
                coef[first + i, :, lanes] = (
                    e[first + i, :, lanes] * factor[b:b + 1, :] - at * eye_f
                ).astype(jnp.bfloat16)

    def exchange(p, h):
        return pltpu.make_async_remote_copy(
            src_ref=gk.at[p, h], dst_ref=sib.at[p],
            send_sem=x_send.at[p], recv_sem=x_recv.at[p],
            device_id={"rep": other}, device_id_type=pl.DeviceIdType.MESH)

    def scatter(p, p_dst, to):
        return pltpu.make_async_remote_copy(
            src_ref=outb.at[p], dst_ref=inb.at[p_dst],
            send_sem=s_send.at[p], recv_sem=s_recv.at[p_dst],
            device_id={"dp": to}, device_id_type=pl.DeviceIdType.MESH)

    def key_grad(first, count):
        c = coef[pl.ds(first, count)].reshape(count * tile, rows)
        for g in range(4):
            cols = slice(g * (width // 4), (g + 1) * (width // 4))
            part = scale * jnp.dot(c, q[:, cols], preferred_element_type=jnp.float32)
            gk[pl.ds(first, count), :, :, cols] = part.reshape(count, 2, half, width // 4)

    def gather_sum(p):
        exchange(p, other).wait_recv()
        return gk[p, r] + sib[p]

    def ship(p):
        outb[p] = gather_sum(p).astype(jnp.bfloat16)
        k = jnp.where(p > REACH, p - REACH - 1, p)
        scatter(p, p, jnp.where(k == 1, mate[1], jnp.where(k == 2, mate[2], mate[3]))).start()

    @pl.loop(0, REACH)
    def _(i):
        j = REACH - i
        finish(j, [pick(2 * j - 1), pick(2 * j)], 2 * j - 1)
        key_grad(2 * j - 1, 2)
        for p in (2 * j - 1, 2 * j):
            exchange(p, other).start()
        for p in (2 * j + 1, 2 * j + 2):
            @pl.when((i > 0) & (p != REACH) & (p != REACH + 1))
            def _():
                ship(p)

    finish(0, owners[:1], 0)
    key_grad(0, 1)
    exchange(0, other).start()
    far = [gather_sum(REACH), gather_sum(REACH + 1)]
    for k in (1, 2, 3):
        scatter(REACH + 1 + k, REACH + 1 + k, d).wait_recv()
        part = inb[REACH + 1 + k].astype(jnp.float32)
        far = [far[0] + jnp.where(place[k] > r4, part, 0.0),
               far[1] + jnp.where(place[k] > r4, 0.0, part)]
    for p, p_dst, by in ((REACH, REACH + 1, REACH), (REACH + 1, REACH, -REACH)):
        outb[p] = far[p - REACH].astype(jnp.bfloat16)
        scatter(p, p_dst, dev(by)).start()
    ship(1)
    ship(2)

    k_all = kwin[...].reshape((2 * REACH + 1) * tile, width)
    c_all = coef
    step = rows // 4
    for g in range(4):
        ct = c_all[:, :, g * step:(g + 1) * step].reshape((2 * REACH + 1) * tile, step)
        gq[g * step:(g + 1) * step, :] = scale * lax.dot_general(
            ct, k_all, (((0,), (0,)), ((), ())), preferred_element_type=jnp.float32)

    exchange(0, other).wait_recv()
    acc = gk[0, r] + sib[0]
    for p in range(1, REACH + 2):
        scatter(p, p, d).wait_recv()
        acc = acc + inb[p].astype(jnp.float32)
    gk_out[...] = acc

    exchange(0, other).wait_send()
    for p in range(1, 2 * REACH + 1):
        gather(p, d).wait_send()
        forward(p, r).wait_send()
        exchange(p, other).wait_send()
        scatter(p, p, d).wait_send()


def body(queries, keys, neg_mask, positive, row_weight):
    n = lax.axis_size("dp")
    rows, width = queries.shape
    tile = keys.shape[0]
    blocks = rows // tile
    half = tile // 2
    slots = 2 * REACH + 1
    hbm, vmem, smem = (pl.BlockSpec(memory_space=m) for m in (pltpu.HBM, pltpu.VMEM, pltpu.SMEM))
    f32, bf16 = jnp.float32, jnp.bfloat16
    dma = pltpu.SemaphoreType.DMA
    loss, gq, gk = pl.pallas_call(
        functools.partial(kernel, n),
        out_shape=(
            jax.ShapeDtypeStruct((blocks, tile), f32),
            jax.ShapeDtypeStruct((rows, width), f32),
            jax.ShapeDtypeStruct((half, width), f32),
        ),
        in_specs=[hbm, hbm, hbm, hbm, hbm],
        out_specs=(vmem, vmem, vmem),
        scratch_shapes=[
            pltpu.SMEM(neg_mask.shape, jnp.int32),
            pltpu.SMEM(positive.shape, jnp.int32),
            pltpu.VMEM((blocks, tile), f32),
            pltpu.VMEM((rows, width), bf16),
            pltpu.VMEM((slots, 2, half, width), bf16),
            pltpu.VMEM((slots, tile, rows), f32),
            pltpu.VMEM((slots, tile, rows), bf16),
            pltpu.VMEM((slots, 2, half, width), f32),
            pltpu.VMEM((slots, half, width), f32),
            pltpu.VMEM((slots, half, width), bf16),
            pltpu.VMEM((slots, half, width), bf16),
            pltpu.VMEM((blocks, tile), f32),
            pltpu.VMEM((blocks, tile), f32),
            pltpu.VMEM((blocks, tile), f32),
            pltpu.VMEM((REACH + 1, blocks, tile), f32),
            dma((6,)),
            dma((slots,)), dma((slots,)), dma((slots,)), dma((slots,)),
            dma((slots,)), dma((slots,)), dma((slots,)), dma((slots,)),
        ],
        compiler_params=pltpu.CompilerParams(
            collective_id=0, has_side_effects=True, vmem_limit_bytes=40 * 1024 * 1024),
        cost_estimate=pl.CostEstimate(
            flops=6 * rows * slots * tile * width, bytes_accessed=8 * rows * width,
            transcendentals=rows * slots * tile),
    )(queries, keys, neg_mask, positive, row_weight.reshape(blocks, tile))
    return loss.reshape(rows), gq, gk


def solution(mesh):
    placed = (
        P(("dp", "rep"), None),
        P("dp", None),
        P(("dp", "rep"), None),
        P(("dp", "rep")),
        P(("dp", "rep")),
    )
    return jax.shard_map(
        body,
        mesh=mesh,
        in_specs=placed,
        out_specs=(P(("dp", "rep")), P(("dp", "rep"), None), P(("dp", "rep"), None)),
        check_vma=False,
    )
```

time: 62.4 us -> 51.5 us (0.83)
  Pallas kernels: 50.8 us -> 42.7 us
  local copies, waits for them, and re-layouts: 10.6 us -> 7.87 us
    pallas_call x1, Pallas kernels: 50.8 us -> 42.7 us  [body(): pl.pallas_call(functools.partial(kernel, n), out_shape=(jax.ShapeDtypeStr...]
    unnamed x13, local copies, waits for them, and re-layouts: 10.6 us -> 7.87 us
where the time goes in v2:
time: 51.5 us; the launch traced here: 51.2 us
  Pallas kernels  42.7 us (83%)
  local copies, waits for them, and re-layouts  7.87 us (15%)
  between operations  0.65 us (1%)
    pallas_call x1, Pallas kernels, body(): pl.pallas_call(functools.partial(kernel, n), out_shape=(jax.ShapeDtypeStr...  42.7 us
    unnamed x13, local copies, waits for them, and re-layouts  7.87 us

profile of v2, /device:TPU:0, one launch (start us, length us, event | category | flops | bytes accessed | tf_op | source)
XLA Modules:
  0.0 51.2 jit_solution(7322443165929769018)
XLA Ops:
  0.6 0.0 copy-start
  0.6 1.6 %copy-done = bf16[1024,1024]{1,0:T(8,128)(2,1)S(1)} copy-done((bf16[1024,1024]{1,0:T(8,128)(2,1)S(1)}, bf16[1024,1024]{1,0:T(8,128)(2,1)}, u32[]{:S(2)}) %copy-start) | copy-done | bytes 2097176
  2.2 0.0 copy-start.1
  2.2 0.9 %copy-done.1 = bf16[128,1024]{1,0:T(8,128)(2,1)S(1)} copy-done((bf16[128,1024]{1,0:T(8,128)(2,1)S(1)}, bf16[128,1024]{1,0:T(8,128)(2,1)}, u32[]{:S(2)}) %copy-start.1) | copy-done | bytes 262168
  3.2 0.0 copy-start.2
  3.2 0.7 %copy-done.2 = s32[8,16]{1,0:T(8,128)S(1)} copy-done((s32[8,16]{1,0:T(8,128)S(1)}, s32[8,16]{1,0:T(8,128)}, u32[]{:S(2)}) %copy-start.2) | copy-done | bytes 536
  3.9 0.0 copy-start.3
  3.9 0.7 %copy-done.3 = f32[1024]{0:T(1024)S(1)} copy-done((f32[1024]{0:T(1024)S(1)}, f32[1024]{0:T(1024)}, u32[]{:S(2)}) %copy-start.3) | copy-done | bytes 4120
  4.5 0.0 copy-start.4
  4.6 0.7 %copy-done.4 = s32[8]{0:T(128)S(1)} copy-done((s32[8]{0:T(128)S(1)}, s32[8]{0:T(128)}, u32[]{:S(2)}) %copy-start.4) | copy-done | bytes 56
  5.2 42.7 %shard_map.76 = (f32[8,128]{1,0:T(8,128)S(1)}, f32[1024,1024]{1,0:T(8,128)S(1)}, f32[64,1024]{1,0:T(8,128)S(1)}) custom-call(bf16[1024,1024]{1,0:T(8,128)(2,1)S(1)} %copy-done, bf16[128,1024]{1,0:T(8,128)(2,1)S(1)} %copy-done.1, s32[8,16]{1,0:T(8,128)S(1)} %copy-done.2, s32[8]{0:T(128)S(1)} %copy-done.4, f32[8,128]{1,0:T(8,128)S(1)} %bitcast.3), custom_call_target="tpu_custom_call" | custom-call | flops 7247757312 | bytes 8388608 | tf_op jit(solution)/shard_map/pallas_call | solution.py:269
  47.9 0.6 %copy.11 = f32[1024]{0:T(1024)} copy(f32[1024]{0:T(1024)S(1)} %bitcast.2) | data formatting | bytes 8192
  48.5 2.0 %copy.12 = f32[1024,1024]{1,0:T(8,128)} copy(f32[1024,1024]{1,0:T(8,128)S(1)} %get-tuple-element.13) | data formatting | bytes 8388608
  50.5 0.7 %copy.13 = f32[64,1024]{1,0:T(8,128)} copy(f32[64,1024]{1,0:T(8,128)S(1)} %get-tuple-element.14) | data formatting | bytes 524288
Async XLA Ops:
  0.6 1.6 %copy-start = (bf16[1024,1024]{1,0:T(8,128)(2,1)S(1)}, bf16[1024,1024]{1,0:T(8,128)(2,1)}, u32[]{:S(2)}) copy-start(bf16[1024,1024]{1,0:T(8,128)(2,1)} %q_hbm.1) | copy-start | bytes 6291460
  2.2 0.9 %copy-start.1 = (bf16[128,1024]{1,0:T(8,128)(2,1)S(1)}, bf16[128,1024]{1,0:T(8,128)(2,1)}, u32[]{:S(2)}) copy-start(bf16[128,1024]{1,0:T(8,128)(2,1)} %k_hbm.1) | copy-start | bytes 786436
  3.2 0.7 %copy-start.2 = (s32[8,16]{1,0:T(8,128)S(1)}, s32[8,16]{1,0:T(8,128)}, u32[]{:S(2)}) copy-start(s32[8,16]{1,0:T(8,128)} %mask_hbm.1) | copy-start | bytes 1540
  3.9 0.7 %copy-start.3 = (f32[1024]{0:T(1024)S(1)}, f32[1024]{0:T(1024)}, u32[]{:S(2)}) copy-start(f32[1024]{0:T(1024)} %param.9) | copy-start | bytes 12292
  4.5 0.7 %copy-start.4 = (s32[8]{0:T(128)S(1)}, s32[8]{0:T(128)}, u32[]{:S(2)}) copy-start(s32[8]{0:T(128)} %pos_hbm.1) | copy-start | bytes 100

commit v3 on v2

--- a/solution.py
+++ b/solution.py
@@ -74,6 +74,12 @@
             send_sem=g_send.at[REACH + 1 + k], recv_sem=g_recv.at[REACH + 1 + k],
             device_id={"dp": mate[k]}, device_id_type=pl.DeviceIdType.MESH)
 
+    def across():
+        return pltpu.make_async_remote_copy(
+            src_ref=kwin.at[via, r], dst_ref=kwin.at[3, r],
+            send_sem=g_send.at[3], recv_sem=g_recv.at[3],
+            device_id={"dp": mate_last}, device_id_type=pl.DeviceIdType.MESH)
+
     def pass_on(src):
         gather(src, d).wait_recv()
         for k in (1, 2, 3):
@@ -90,8 +96,11 @@
 
     gather(REACH + 1, dev(REACH)).start()
     gather(REACH, dev(-REACH)).start()
-    for k in (1, 2, 3):
-        gather(k, mate[k]).start()
+    via = 1 + r
+    mate_via = jnp.where(via == 1, mate[1], mate[2])
+    mate_last = jnp.where(via == 1, mate[2], mate[1])
+    gather(via, mate_via).start()
+    gather(3 - via, mate_last).start()
 
     run_max[...] = jnp.full(run_max.shape, NEG, jnp.float32)
     run_sum[...] = jnp.zeros(run_sum.shape, jnp.float32)
@@ -144,6 +153,9 @@
             out = jnp.where(p == i, owners[i], out)
         return out
 
+    gather(via, d).wait_recv()
+    across().start()
+    forward(via, r).start()
     near = jnp.where(d + REACH < n, REACH, REACH + 1)
     pass_on(near)
 
@@ -156,7 +168,7 @@
             pass_on(2 * REACH + 1 - near)
 
         for p in pair:
-            @pl.when((p != REACH) & (p != REACH + 1))
+            @pl.when((p != REACH) & (p != REACH + 1) & (p != via))
             def _():
                 gather(p, d).wait_recv()
                 forward(p, r).start()

time: 51.5 us -> 51.2 us (level)
  no operation moved by 1% of the time
where the time goes in v3:
time: 51.2 us; the launch traced here: 51 us
  Pallas kernels  42.5 us (83%)
  local copies, waits for them, and re-layouts  7.87 us (15%)
  between operations  0.65 us (1%)
    pallas_call x1, Pallas kernels, body(): pl.pallas_call(functools.partial(kernel, n), out_shape=(jax.ShapeDtypeStr...  42.5 us
    unnamed x13, local copies, waits for them, and re-layouts  7.87 us

profile of v3, /device:TPU:0, one launch (start us, length us, event | category | flops | bytes accessed | tf_op | source)
XLA Modules:
  0.0 51.0 jit_solution(5809097991147835213)
XLA Ops:
  0.6 0.0 copy-start
  0.6 1.6 %copy-done = bf16[1024,1024]{1,0:T(8,128)(2,1)S(1)} copy-done((bf16[1024,1024]{1,0:T(8,128)(2,1)S(1)}, bf16[1024,1024]{1,0:T(8,128)(2,1)}, u32[]{:S(2)}) %copy-start) | copy-done | bytes 2097176
  2.2 0.0 copy-start.1
  2.2 0.9 %copy-done.1 = bf16[128,1024]{1,0:T(8,128)(2,1)S(1)} copy-done((bf16[128,1024]{1,0:T(8,128)(2,1)S(1)}, bf16[128,1024]{1,0:T(8,128)(2,1)}, u32[]{:S(2)}) %copy-start.1) | copy-done | bytes 262168
  3.2 0.0 copy-start.2
  3.2 0.7 %copy-done.2 = s32[8,16]{1,0:T(8,128)S(1)} copy-done((s32[8,16]{1,0:T(8,128)S(1)}, s32[8,16]{1,0:T(8,128)}, u32[]{:S(2)}) %copy-start.2) | copy-done | bytes 536
  3.9 0.0 copy-start.3
  3.9 0.7 %copy-done.3 = f32[1024]{0:T(1024)S(1)} copy-done((f32[1024]{0:T(1024)S(1)}, f32[1024]{0:T(1024)}, u32[]{:S(2)}) %copy-start.3) | copy-done | bytes 4120
  4.5 0.0 copy-start.4
  4.6 0.7 %copy-done.4 = s32[8]{0:T(128)S(1)} copy-done((s32[8]{0:T(128)S(1)}, s32[8]{0:T(128)}, u32[]{:S(2)}) %copy-start.4) | copy-done | bytes 56
  5.2 42.5 %shard_map.76 = (f32[8,128]{1,0:T(8,128)S(1)}, f32[1024,1024]{1,0:T(8,128)S(1)}, f32[64,1024]{1,0:T(8,128)S(1)}) custom-call(bf16[1024,1024]{1,0:T(8,128)(2,1)S(1)} %copy-done, bf16[128,1024]{1,0:T(8,128)(2,1)S(1)} %copy-done.1, s32[8,16]{1,0:T(8,128)S(1)} %copy-done.2, s32[8]{0:T(128)S(1)} %copy-done.4, f32[8,128]{1,0:T(8,128)S(1)} %bitcast.3), custom_call_target="tpu_custom_call" | custom-call | flops 7247757312 | bytes 8388608 | tf_op jit(solution)/shard_map/pallas_call | solution.py:281
  47.7 0.6 %copy.11 = f32[1024]{0:T(1024)} copy(f32[1024]{0:T(1024)S(1)} %bitcast.2) | data formatting | bytes 8192
  48.3 2.0 %copy.12 = f32[1024,1024]{1,0:T(8,128)} copy(f32[1024,1024]{1,0:T(8,128)S(1)} %get-tuple-element.13) | data formatting | bytes 8388608
  50.3 0.7 %copy.13 = f32[64,1024]{1,0:T(8,128)} copy(f32[64,1024]{1,0:T(8,128)S(1)} %get-tuple-element.14) | data formatting | bytes 524288
Async XLA Ops:
  0.6 1.6 %copy-start = (bf16[1024,1024]{1,0:T(8,128)(2,1)S(1)}, bf16[1024,1024]{1,0:T(8,128)(2,1)}, u32[]{:S(2)}) copy-start(bf16[1024,1024]{1,0:T(8,128)(2,1)} %q_hbm.1) | copy-start | bytes 6291460
  2.2 0.9 %copy-start.1 = (bf16[128,1024]{1,0:T(8,128)(2,1)S(1)}, bf16[128,1024]{1,0:T(8,128)(2,1)}, u32[]{:S(2)}) copy-start(bf16[128,1024]{1,0:T(8,128)(2,1)} %k_hbm.1) | copy-start | bytes 786436
  3.2 0.7 %copy-start.2 = (s32[8,16]{1,0:T(8,128)S(1)}, s32[8,16]{1,0:T(8,128)}, u32[]{:S(2)}) copy-start(s32[8,16]{1,0:T(8,128)} %mask_hbm.1) | copy-start | bytes 1540
  3.9 0.7 %copy-start.3 = (f32[1024]{0:T(1024)S(1)}, f32[1024]{0:T(1024)}, u32[]{:S(2)}) copy-start(f32[1024]{0:T(1024)} %param.9) | copy-start | bytes 12292
  4.5 0.7 %copy-start.4 = (s32[8]{0:T(128)S(1)}, s32[8]{0:T(128)}, u32[]{:S(2)}) copy-start(s32[8]{0:T(128)} %pos_hbm.1) | copy-start | bytes 100

commit v4 on v3

--- a/solution.py
+++ b/solution.py
@@ -13,9 +13,9 @@
 NEG = -1e30
 
 
-def kernel(n, q_hbm, k_hbm, mask_hbm, pos_hbm, weight_hbm, loss, gq, gk_out,
-           mask, positive, weight, q, kwin, e, coef, gk, sib, outb, inb, run_max, run_sum, pos_logit, hist,
-           local_sem, g_send, g_recv, f_send, f_recv, x_send, x_recv, s_send, s_recv):
+def kernel(n, q_hbm, k_hbm, mask_hbm, pos_hbm, weight_hbm, loss, gq_hbm, gk_out,
+           mask, positive, weight, q, kwin, e, coef, gk, sib, outb, inb, gq, run_max, run_sum, pos_logit, hist,
+           local_sem, g_send, g_recv, f_send, f_recv, x_send, x_recv, s_send, s_recv, o_sem):
     rows, width = q.shape
     blocks, tile = weight.shape
     half = tile // 2
@@ -245,6 +245,10 @@
     ship(1)
     ship(2)
 
+    def give(g):
+        part = pl.ds(g * (rows // 4), rows // 4)
+        return pltpu.make_async_copy(gq.at[part], gq_hbm.at[part], o_sem.at[g])
+
     k_all = kwin[...].reshape((2 * REACH + 1) * tile, width)
     c_all = coef
     step = rows // 4
@@ -252,6 +256,7 @@
         ct = c_all[:, :, g * step:(g + 1) * step].reshape((2 * REACH + 1) * tile, step)
         gq[g * step:(g + 1) * step, :] = scale * lax.dot_general(
             ct, k_all, (((0,), (0,)), ((), ())), preferred_element_type=jnp.float32)
+        give(g).start()
 
     exchange(0, other).wait_recv()
     acc = gk[0, r] + sib[0]
@@ -259,6 +264,8 @@
         scatter(p, p, d).wait_recv()
         acc = acc + inb[p].astype(jnp.float32)
     gk_out[...] = acc
+    for g in range(4):
+        give(g).wait()
 
     exchange(0, other).wait_send()
     for p in range(1, 2 * REACH + 1):
@@ -286,7 +293,7 @@
             jax.ShapeDtypeStruct((half, width), f32),
         ),
         in_specs=[hbm, hbm, hbm, hbm, hbm],
-        out_specs=(vmem, vmem, vmem),
+        out_specs=(vmem, hbm, vmem),
         scratch_shapes=[
             pltpu.SMEM(neg_mask.shape, jnp.int32),
             pltpu.SMEM(positive.shape, jnp.int32),
@@ -299,6 +306,7 @@
             pltpu.VMEM((slots, half, width), f32),
             pltpu.VMEM((slots, half, width), bf16),
             pltpu.VMEM((slots, half, width), bf16),
+            pltpu.VMEM((rows, width), f32),
             pltpu.VMEM((blocks, tile), f32),
             pltpu.VMEM((blocks, tile), f32),
             pltpu.VMEM((blocks, tile), f32),
@@ -306,9 +314,10 @@
             dma((6,)),
             dma((slots,)), dma((slots,)), dma((slots,)), dma((slots,)),
             dma((slots,)), dma((slots,)), dma((slots,)), dma((slots,)),
+            dma((4,)),
         ],
         compiler_params=pltpu.CompilerParams(
-            collective_id=0, has_side_effects=True, vmem_limit_bytes=40 * 1024 * 1024),
+            collective_id=0, has_side_effects=True, vmem_limit_bytes=58 * 1024 * 1024),
         cost_estimate=pl.CostEstimate(
             flops=6 * rows * slots * tile * width, bytes_accessed=8 * rows * width,
             transcendentals=rows * slots * tile),

time: 51.2 us -> 50.7 us (level)
  local copies, waits for them, and re-layouts: 7.87 us -> 6.81 us
  Pallas kernels: 42.5 us -> 43.1 us
    unnamed x13 -> x5, local copies, waits for them, and re-layouts: 7.87 us -> 6.81 us
    pallas_call x1, Pallas kernels: 42.5 us -> 43.1 us  [body(): pl.pallas_call(functools.partial(kernel, n), out_shape=(jax.ShapeDtypeStr...]
where the time goes in v4:
time: 50.7 us; the launch traced here: 50.5 us
  Pallas kernels  43.1 us (85%)
  local copies, waits for them, and re-layouts  6.81 us (13%)
  between operations  0.64 us (1%)
    pallas_call x1, Pallas kernels, body(): pl.pallas_call(functools.partial(kernel, n), out_shape=(jax.ShapeDtypeStr...  43.1 us
    unnamed x5, local copies, waits for them, and re-layouts  6.81 us

profile of v4, /device:TPU:0, one launch (start us, length us, event | category | flops | bytes accessed | tf_op | source)
XLA Modules:
  0.0 50.5 jit_solution(2618120135305924627)
XLA Ops:
  0.6 43.1 %shard_map.76 = (f32[8,128]{1,0:T(8,128)}, f32[1024,1024]{1,0:T(8,128)}, f32[64,1024]{1,0:T(8,128)}) custom-call(bf16[1024,1024]{1,0:T(8,128)(2,1)} %q_hbm.1, bf16[128,1024]{1,0:T(8,128)(2,1)} %k_hbm.1, s32[8,16]{1,0:T(8,128)} %mask_hbm.1, s32[8]{0:T(128)} %pos_hbm.1, f32[8,128]{1,0:T(8,128)} %bitcast.3), custom_call_target="tpu_custom_call" | custom-call | flops 7247757312 | bytes 8388608 | tf_op jit(solution)/shard_map/pallas_call | solution.py:288
  43.7 1.3 %copy.11 = f32[1024]{0:T(1024)} copy(f32[1024]{0:T(1024)} %bitcast.2) | data formatting | bytes 8192
  45.0 0.0 copy-start
  45.0 4.8 %copy.12 = f32[1024,1024]{1,0:T(8,128)} copy(f32[1024,1024]{1,0:T(8,128)} %get-tuple-element.13) | data formatting | bytes 8388608
  49.8 0.0 copy-done
  49.8 0.7 %copy.13 = f32[64,1024]{1,0:T(8,128)} copy(f32[64,1024]{1,0:T(8,128)S(1)} %copy-done) | data formatting | bytes 524288
Async XLA Ops:
  45.0 4.8 %copy-start = (f32[64,1024]{1,0:T(8,128)S(1)}, f32[64,1024]{1,0:T(8,128)}, u32[]{:S(2)}) copy-start(f32[64,1024]{1,0:T(8,128)} %get-tuple-element.14) | copy-start | bytes 786436
